TPU v7x, 128 devices: a whole 4x4x4 slice. The times are simulated.
128 devices in a mesh: shot: 16 (over z_hi, x, core), slab: 8 (over y, z_lo).
Axes of the slice: x: 4, y: 4, z: 4 (z_hi: 2, z_lo: 2; z = z_hi * 2 + z_lo), core: 2. Of those that a mesh axis runs over, the one named last changes fastest.
Arguments:
- kappa: float32 [128, 256, 256], P('slab', 'shot'), may hold values from 0.05 to 0.25
- buoyancy: float32 [128, 256, 256], P('slab', 'shot'), may hold values from 0.5 to 1
- anchors: int32 [16, 2], replicated, may hold values from 0 to 128
- wave_start: float32 [16, 2, 128, 128, 128], P('shot', None, 'slab'), may hold values from -1.8 to 1.8
- adjoint_start: float32 [16, 2, 128, 128, 128], P('shot', None, 'slab'), may hold values from -1.8 to 1.8
- wavelet: float32 [16, 4], P('shot'), may hold values from -4 to 4
- source_cell: int32 [16, 3], P('shot'), may hold values from 0 to 127
- receiver_cells: int32 [16, 512, 3], P('shot'), may hold values from 0 to 127
- observed: float32 [16, 4, 512], P('shot'), may hold values from -3 to 3
Outputs:
- model_grad: float32 [128, 256, 256], P('slab', 'shot')
- wave_end: float32 [16, 2, 128, 128, 128], P('shot', None, 'slab')
- adjoint_end: float32 [16, 2, 128, 128, 128], P('shot', None, 'slab')
Inputs may be any that keep to these rules, and one draw needn't show every extreme that they name: `anchors`: apertures lie inside the model; several shots' apertures may cover the same cells. `receiver_cells`: several receivers may share a cell.
All inputs are finite; a program needn't handle non-finite values.
Results may differ from a plain program's by a relative error of at most 0.00002.
Values sent between devices are 32-bit elements; how exact they have to be, the bound alone decides.
A program may use at most 128 MiB of HBM per device.

v0:
```python
import jax
import jax.numpy as jnp
from jax import lax
from jax.sharding import PartitionSpec as P

NT = 4


def with_halo(array, sides, width):
    for axis, dim in sides:
        count, length = (lax.axis_size(axis), array.shape[dim])
        up = [(i, (i + 1) % count) for i in range(count - 1)]
        down = [(j, i) for i, j in up]
        last = lax.slice_in_dim(array, length - width, length, axis=dim)
        first = lax.slice_in_dim(array, 0, width, axis=dim)
        before = lax.ppermute(last, axis, up)
        after = lax.ppermute(first, axis, down)
        array = jnp.concatenate([before, array, after], axis=dim)
    return array


def spread_of(field, faces):
    depth_face, row_face, col_face = faces
    pad_depth = with_halo(field, (("slab", 0),), 1)
    flux = depth_face * (pad_depth[1:] - pad_depth[:-1])
    result = flux[1:] - flux[:-1]
    pad_rows = jnp.pad(field, ((0, 0), (1, 1), (0, 0)))
    flux = row_face * (pad_rows[:, 1:] - pad_rows[:, :-1])
    result = result + (flux[:, 1:] - flux[:, :-1])
    pad_cols = jnp.pad(field, ((0, 0), (0, 0), (1, 1)))
    flux = col_face * (pad_cols[:, :, 1:] - pad_cols[:, :, :-1])
    return result + (flux[:, :, 1:] - flux[:, :, :-1])


def add_cells(field, positions, amounts):
    shape = field.shape
    return field.reshape(-1).at[positions].add(amounts).reshape(shape)


def shards(
    kappa,
    buoyancy,
    anchors,
    wave_start,
    adjoint_start,
    wavelet,
    source_cell,
    receiver_cells,
    observed,
):
    depth_cells = kappa.shape[0]
    own_rows = kappa.shape[1]
    model_side = kappa.shape[2]
    aperture = wave_start.shape[3]
    groups = lax.axis_size("shot")
    shot_index = lax.axis_index("shot")
    anchor = anchors[shot_index]
    row_anchor = anchor[0]
    col_anchor = anchor[1]
    stacked = jnp.stack([kappa, buoyancy])
    gathered = lax.all_gather(stacked, "shot", axis=2, tiled=True)
    window = lax.dynamic_slice(
        gathered,
        (row_anchor * 0, row_anchor * 0, row_anchor, col_anchor),
        (2, depth_cells, aperture, aperture),
    )
    kappa_window = window[0]
    buoy_window = window[1]
    padded_buoy = with_halo(buoy_window, (("slab", 0),), 1)
    depth_face = 0.5 * (padded_buoy[1:] + padded_buoy[:-1])
    pad_rows = jnp.pad(buoy_window, ((0, 0), (1, 1), (0, 0)))
    pad_cols = jnp.pad(buoy_window, ((0, 0), (0, 0), (1, 1)))
    row_face = 0.5 * (pad_rows[:, 1:] + pad_rows[:, :-1])
    col_face = 0.5 * (pad_cols[:, :, 1:] + pad_cols[:, :, :-1])
    faces = (depth_face, row_face, col_face)
    depth_start = lax.axis_index("slab") * depth_cells
    receivers = receiver_cells[0]
    local_depth = receivers[:, 0] - depth_start
    receiver_valid = (local_depth >= 0) & (local_depth < depth_cells)
    receiver_flat = (
        jnp.clip(local_depth, 0, depth_cells - 1) * aperture + receivers[:, 1]
    ) * aperture + receivers[:, 2]
    source = source_cell[0]
    source_depth = source[0] - depth_start
    source_valid = (source_depth >= 0) & (source_depth < depth_cells)
    source_flat = (
        jnp.clip(source_depth, 0, depth_cells - 1) * aperture + source[1]
    ) * aperture + source[2]
    before = wave_start[0, 0]
    current = wave_start[0, 1]
    spreads = []
    residuals = []
    for moment in range(NT):
        spread = spread_of(current, faces)
        spreads.append(spread)
        following = 2.0 * current - before + kappa_window * spread
        following = add_cells(
            following, source_flat[None], jnp.where(source_valid, wavelet[0, moment], 0.0)[None]
        )
        sampled = following.reshape(-1)[receiver_flat]
        residuals.append(jnp.where(receiver_valid, sampled - observed[0, moment], 0.0))
        before = current
        current = following
    after = adjoint_start[0, 0]
    later = adjoint_start[0, 1]
    imaging = None
    for moment in reversed(range(NT)):
        adjoint_now = 2.0 * later - after + spread_of(kappa_window * later, faces)
        adjoint_now = add_cells(adjoint_now, receiver_flat, residuals[moment])
        term = adjoint_now * spreads[moment]
        imaging = term if imaging is None else imaging + term
        after = later
        later = adjoint_now
    embedded = lax.dynamic_update_slice(
        jnp.zeros((depth_cells, own_rows * groups, model_side), jnp.float32),
        imaging,
        (row_anchor * 0, row_anchor, col_anchor),
    )
    gradient_rows = lax.psum_scatter(embedded, "shot", scatter_dimension=1, tiled=True)
    return (gradient_rows, jnp.stack([before, current])[None], jnp.stack([after, later])[None])


def solution(mesh):
    in_specs = (
        P("slab", "shot", None),
        P("slab", "shot", None),
        P(),
        P("shot", None, "slab", None, None),
        P("shot", None, "slab", None, None),
        P("shot", None),
        P("shot", None),
        P("shot", None, None),
        P("shot", None, None),
    )
    out_specs = (
        P("slab", "shot", None),
        P("shot", None, "slab", None, None),
        P("shot", None, "slab", None, None),
    )
    return jax.shard_map(shards, mesh=mesh, in_specs=in_specs, out_specs=out_specs, check_vma=False)
```

profile of v0, /device:TPU:0, one launch (start us, length us, event | category | flops | bytes accessed | tf_op | source)
XLA Modules:
  0.0 375.5 jit_solution(16419638537728177638)
XLA Ops:
  7.3 1.9 pad_maximum_fusion
  10.1 3.9 %collective-permute-start.5 = (f32[1,128,128]{2,1,0:T(8,128)S(1)}, f32[1,128,128]{2,1,0:T(8,128)S(1)}, u32[]{:S(2)}, u32[]{:S(2)}) collective-permute-start(f32[1,128,128]{2,1,0:T(8,128)S(1)} %get-tuple-element.66), channel_id=1, source_target_pairs={{0,1},{1,2},{2,3},{3,4},{4,5},{5,6},{6,7},{8,9},{9,10},{10,11},{11... | collective-permute-start | bytes 196616 | tf_op jit(solution)/shard_map/ppermute | solution.py:16
  27.3 2.3 slice_bitcast_fusion
  29.6 56.8 %all-gather.2.cloned.1.call-done = f32[2,16,256,256]{3,2,1,0:T(8,128)} async-done(((f32[2,16,16,256]{3,2,1,0:T(8,128)}), f32[2,16,256,256]{3,2,1,0:T(8,128)}) %all-gather.2.cloned.1.call-update) | async-done | bytes 8388624 | tf_op jit(solution)/shard_map/all_gather | solution.py:61
  88.9 4.5 %collective-permute-start.1 = (f32[1,128,128]{2,1,0:T(8,128)S(1)}, f32[1,128,128]{2,1,0:T(8,128)S(1)}, u32[]{:S(2)}, u32[]{:S(2)}) collective-permute-start(f32[1,128,128]{2,1,0:T(8,128)S(1)} %get-tuple-element.65), channel_id=1, source_target_pairs={{0,1},{1,2},{2,3},{3,4},{4,5},{5,6},{6,7},{8,9},{9,10},{10,11},{11... | collective-permute-start | bytes 196616 | tf_op jit(solution)/shard_map/ppermute | solution.py:16
  93.4 2.0 dynamic-slice_bitcast_fusion.1
  97.1 1.8 copy-done.30
  98.9 3.6 fusion.47
  103.3 3.5 collective-permute-start.7
  108.1 2.0 fusion.7
  111.2 7.9 %gather_fusion.3 = f32[512]{0:T(512)} fusion(f32[262144]{0:T(1024)} %copy-done.9, s32[1024]{0:T(1024)S(1)} %pad_clamp_fusion), kind=kCustom, calls=%fused_computation.3 | custom fusion | bytes 6144 | tf_op jit(solution)/shard_map/gather | solution.py:100
  119.1 1.9 fusion.21
  121.3 4.8 %multiply_add_fusion.3 = (f32[16,128,128]{2,1,0:T(8,128)S(1)}, f32[16,128,128]{2,1,0:T(8,128)}) fusion(f32[16,128,128]{2,1,0:T(8,128)S(1)} %bitcast.114, f32[2,16,256,256]{3,2,1,0:T(8,128)} %all-gather.2.cloned.1.call-done, s32[]{:T(128)S(6)} %select_n.55, s32[]{:T(128)S(6)} %select_n.56, f32[1,2,16,128,128]{4,3,2,1,0:T(8,128)} %param.20, ...), kind=kLoop, calls=%fused_computation.128 | loop fusion | flops 2359296 | bytes 11534344 | tf_op jit(solution)/shard_map/add | solution.py:96
  127.0 4.4 %collective-permute-start.9 = (f32[1,128,128]{2,1,0:T(8,128)S(1)}, f32[1,128,128]{2,1,0:T(8,128)S(1)}, u32[]{:S(2)}, u32[]{:S(2)}) collective-permute-start(f32[1,128,128]{2,1,0:T(8,128)S(1)} %get-tuple-element.76), channel_id=1, source_target_pairs={{0,1},{1,2},{2,3},{3,4},{4,5},{5,6},{6,7},{8,9},{9,10},{10,11},{11... | collective-permute-start | bytes 196616 | tf_op jit(solution)/shard_map/ppermute | solution.py:16
  132.6 2.0 fusion.9
  135.8 8.0 %gather_fusion.2 = f32[512]{0:T(512)} fusion(f32[262144]{0:T(1024)} %copy-done.12, s32[1024]{0:T(1024)S(1)} %pad_clamp_fusion), kind=kCustom, calls=%fused_computation.2 | custom fusion | bytes 6144 | tf_op jit(solution)/shard_map/gather | solution.py:100
  143.8 1.9 fusion.22
  146.3 4.5 %multiply_add_fusion.2 = (f32[16,128,128]{2,1,0:T(8,128)S(1)}, f32[16,128,128]{2,1,0:T(8,128)}) fusion(f32[16,128,128]{2,1,0:T(8,128)S(1)} %bitcast.115, f32[16,128,128]{2,1,0:T(8,128)S(1)} %bitcast.120, f32[2,16,256,256]{3,2,1,0:T(8,128)} %all-gather.2.cloned.1.call-done, s32[]{:T(128)S(6)} %select_n.55, s32[]{:T(128)S(6)} %select_n.56, ...), kind=kLoop, calls=%fused_computation.127 | loop fusion | flops 2359296 | bytes 11534344 | tf_op jit(solution)/shard_map/add | solution.py:96
  151.6 4.4 %collective-permute-start.11 = (f32[1,128,128]{2,1,0:T(8,128)S(1)}, f32[1,128,128]{2,1,0:T(8,128)S(1)}, u32[]{:S(2)}, u32[]{:S(2)}) collective-permute-start(f32[1,128,128]{2,1,0:T(8,128)S(1)} %get-tuple-element.74), channel_id=1, source_target_pairs={{0,1},{1,2},{2,3},{3,4},{4,5},{5,6},{6,7},{8,9},{9,10},{10,11},{11... | collective-permute-start | bytes 196616 | tf_op jit(solution)/shard_map/ppermute | solution.py:16
  157.5 2.0 fusion.11
  160.7 7.9 %gather_fusion.1 = f32[512]{0:T(512)} fusion(f32[262144]{0:T(1024)} %copy-done.15, s32[1024]{0:T(1024)S(1)} %pad_clamp_fusion), kind=kCustom, calls=%fused_computation.1 | custom fusion | bytes 6144 | tf_op jit(solution)/shard_map/gather | solution.py:100
  168.6 1.9 fusion.23
  171.1 5.4 %multiply_add_fusion.1 = (f32[16,128,128]{2,1,0:T(8,128)}, f32[16,128,128]{2,1,0:T(8,128)}, f32[16,128,128]{2,1,0:T(8,128)S(1)}) fusion(f32[16,128,128]{2,1,0:T(8,128)S(1)} %bitcast.121, f32[16,128,128]{2,1,0:T(8,128)S(1)} %bitcast.126, f32[2,16,256,256]{3,2,1,0:T(8,128)} %all-gather.2.cloned.1.call-done, s32[]{:T(128)S(6)} %select_n.55, s32[]{:T(128)S(6)} %select_n.56, ...), kind=kLoop, calls=%fused_computation.126 | loop fusion | flops 2621440 | bytes 13631496 | tf_op jit(solution)/shard_map/add | solution.py:96
  177.8 2.0 fusion.3
  179.8 2.1 fusion.55
  182.0 6.5 %gather_fusion = f32[512]{0:T(512)S(1)} fusion(f32[262144]{0:T(1024)} %fusion.55, s32[1024]{0:T(1024)S(1)} %pad_clamp_fusion), kind=kCustom, calls=%fused_computation | custom fusion | bytes 6144 | tf_op jit(solution)/shard_map/gather | solution.py:100
  188.4 5.0 %collective-permute-start.3 = (f32[1,128,128]{2,1,0:T(8,128)S(1)}, f32[1,128,128]{2,1,0:T(8,128)S(1)}, u32[]{:S(2)}, u32[]{:S(2)}) collective-permute-start(f32[1,128,128]{2,1,0:T(8,128)S(1)} %get-tuple-element.80), channel_id=1, source_target_pairs={{0,1},{1,2},{2,3},{3,4},{4,5},{5,6},{6,7},{8,9},{9,10},{10,11},{11... | collective-permute-start | bytes 196616 | tf_op jit(solution)/shard_map/ppermute | solution.py:16
  195.3 5.0 %collective-permute-done.2 = f32[1,128,128]{2,1,0:T(8,128)S(1)} collective-permute-done((f32[1,128,128]{2,1,0:T(8,128)S(1)}, f32[1,128,128]{2,1,0:T(8,128)S(1)}, u32[]{:S(2)}, u32[]{:S(2)}) %collective-permute-start.2) | collective-permute-done | bytes 65568 | tf_op jit(solution)/shard_map/ppermute | solution.py:17
  200.4 1.8 fusion.19
  202.2 3.1 fusion.45
  205.3 5.2 %scatter_fusion = f32[262144]{0:T(1024)} fusion(f32[262144]{0:T(1024)} %bitcast.128, s32[512]{0:T(512)S(1)} %bitcast.149, f32[512]{0:T(512)S(1)} %get-tuple-element.91), kind=kCustom, calls=%fused_computation.4 | custom fusion | flops 512 | bytes 8192 | tf_op jit(solution)/shard_map/scatter-add | solution.py:37
  210.5 2.3 fusion.50
  213.5 4.8 %collective-permute-start.13 = (f32[1,128,128]{2,1,0:T(8,128)S(1)}, f32[1,128,128]{2,1,0:T(8,128)S(1)}, u32[]{:S(2)}, u32[]{:S(2)}) collective-permute-start(f32[1,128,128]{2,1,0:T(8,128)S(1)} %get-tuple-element.72), channel_id=1, source_target_pairs={{0,1},{1,2},{2,3},{3,4},{4,5},{5,6},{6,7},{8,9},{9,10},{10,11},{11... | collective-permute-start | bytes 196616 | tf_op jit(solution)/shard_map/ppermute | solution.py:16
  220.2 4.3 %collective-permute-done.12 = f32[1,128,128]{2,1,0:T(8,128)S(1)} collective-permute-done((f32[1,128,128]{2,1,0:T(8,128)S(1)}, f32[1,128,128]{2,1,0:T(8,128)S(1)}, u32[]{:S(2)}, u32[]{:S(2)}) %collective-permute-start.12) | collective-permute-done | bytes 65568 | tf_op jit(solution)/shard_map/ppermute | solution.py:17
  226.2 5.2 %scatter_fusion.1 = f32[262144]{0:T(1024)} fusion(f32[262144]{0:T(1024)} %bitcast.133, s32[512]{0:T(512)S(1)} %bitcast.150, f32[512]{0:T(512)S(1)} %get-tuple-element.90), kind=kCustom, calls=%fused_computation.5 | custom fusion | flops 512 | bytes 8192 | tf_op jit(solution)/shard_map/scatter-add | solution.py:37
  231.3 2.3 fusion.49
  234.3 2.8 collective-permute-start.15
  239.0 4.3 %collective-permute-done.14 = f32[1,128,128]{2,1,0:T(8,128)S(1)} collective-permute-done((f32[1,128,128]{2,1,0:T(8,128)S(1)}, f32[1,128,128]{2,1,0:T(8,128)S(1)}, u32[]{:S(2)}, u32[]{:S(2)}) %collective-permute-start.14) | collective-permute-done | bytes 65568 | tf_op jit(solution)/shard_map/ppermute | solution.py:17
  245.0 5.2 %scatter_fusion.2 = f32[262144]{0:T(1024)} fusion(f32[262144]{0:T(1024)} %bitcast.138, s32[512]{0:T(512)S(1)} %bitcast.151, f32[512]{0:T(512)S(1)} %get-tuple-element.89), kind=kCustom, calls=%fused_computation.6 | custom fusion | flops 512 | bytes 8192 | tf_op jit(solution)/shard_map/scatter-add | solution.py:37
  250.2 2.3 fusion.48
  253.2 4.8 %collective-permute-start.17 = (f32[1,128,128]{2,1,0:T(8,128)S(1)}, f32[1,128,128]{2,1,0:T(8,128)S(1)}, u32[]{:S(2)}, u32[]{:S(2)}) collective-permute-start(f32[1,128,128]{2,1,0:T(8,128)S(1)} %get-tuple-element.68), channel_id=1, source_target_pairs={{0,1},{1,2},{2,3},{3,4},{4,5},{5,6},{6,7},{8,9},{9,10},{10,11},{11... | collective-permute-start | bytes 196616 | tf_op jit(solution)/shard_map/ppermute | solution.py:16
  259.9 4.3 %collective-permute-done.16 = f32[1,128,128]{2,1,0:T(8,128)S(1)} collective-permute-done((f32[1,128,128]{2,1,0:T(8,128)S(1)}, f32[1,128,128]{2,1,0:T(8,128)S(1)}, u32[]{:S(2)}, u32[]{:S(2)}) %collective-permute-start.16) | collective-permute-done | bytes 65568 | tf_op jit(solution)/shard_map/ppermute | solution.py:17
  265.9 5.3 %scatter_fusion.3 = f32[262144]{0:T(1024)} fusion(f32[262144]{0:T(1024)} %bitcast.143, s32[512]{0:T(512)S(1)} %bitcast.152, f32[512]{0:T(512)S(1)} %get-tuple-element.88), kind=kCustom, calls=%fused_computation.7 | custom fusion | flops 512 | bytes 8192 | tf_op jit(solution)/shard_map/scatter-add | solution.py:37
  271.2 4.3 %multiply_add_fusion = f32[16,128,128]{2,1,0:T(8,128)} fusion(f32[16,128,128]{2,1,0:T(8,128)} %bitcast.144, f32[16,128,128]{2,1,0:T(8,128)} %get-tuple-element.58, f32[16,128,128]{2,1,0:T(8,128)S(1)} %bitcast.141, f32[16,128,128]{2,1,0:T(8,128)} %get-tuple-element.56, f32[16,128,128]{2,1,0:T(8,128)S(1)} %bitcast.137, f32[16,128,128]{2,1,0:T(8,128)} %get-tuple-element.54, ...), kind=kLoop, calls=%fused_computation.125 | loop fusion | flops 1835008 | bytes 9437184 | tf_op jit(solution)/shard_map/add | solution.py:111
  275.5 2.4 broadcast_in_dim.15
  277.9 13.9 %dynamic_update_slice.3 = f32[16,256,256]{2,1,0:T(8,128)} dynamic-update-slice(f32[16,256,256]{2,1,0:T(8,128)} %broadcast_in_dim.15, f32[16,128,128]{2,1,0:T(8,128)S(1)} %copy-done.33, s32[]{:T(128)} %constant.95.clone.1, s32[]{:T(128)S(6)} %select_n.55, s32[]{:T(128)S(6)} %select_n.56) | dynamic-update-slice | bytes 2097156 | tf_op jit(solution)/shard_map/dynamic_update_slice | solution.py:114
  293.0 3.9 %maximum_bitcast_fusion = (f32[1,2,16,128,128]{4,3,2,1,0:T(8,128)}, f32[1,2,16,128,128]{4,3,2,1,0:T(8,128)}) fusion(f32[1,16,128,128]{3,2,1,0:T(8,128)} %bitcast.54, f32[1,16,128,128]{3,2,1,0:T(8,128)S(1)} %bitcast.127, f32[1,16,128,128]{3,2,1,0:T(8,128)} %bitcast.145, f32[1,16,128,128]{3,2,1,0:T(8,128)S(1)} %bitcast.142), kind=kLoop, calls=%fused_computation.44 | loop fusion | flops 1048576 | bytes 8388608 | tf_op jit(solution)/shard_map/broadcast_in_dim | solution.py:120
  296.9 71.7 %reduce-scatter.2.cloned.1.call-done = f32[16,16,256]{2,1,0:T(8,128)} async-done(((f32[16,256,256]{2,1,0:T(8,128)}), f32[16,16,256]{2,1,0:T(8,128)}) %reduce-scatter.2.cloned.1.call-update) | async-done | bytes 262160 | tf_op jit(solution)/shard_map/reduce_scatter | solution.py:119
  (155 shorter events, 37.9 us)
Async XLA Ops:
  7.2 8.1 %copy-start = (s32[16,2]{0,1:T(2,128)S(1)}, s32[16,2]{0,1:T(2,128)}, u32[]{:S(2)}) copy-start(s32[16,2]{0,1:T(2,128)} %param.19) | copy-start | bytes 388
  7.2 11.3 %copy-start.42 = (s32[1,3]{1,0:T(1,128)S(1)}, s32[1,3]{1,0:T(1,128)}, u32[]{:S(2)}) copy-start(s32[1,3]{1,0:T(1,128)} %param.23) | copy-start | bytes 40
  7.2 14.5 %copy-start.35 = (f32[1,4]{1,0:T(1,128)S(1)}, f32[1,4]{1,0:T(1,128)}, u32[]{:S(2)}) copy-start(f32[1,4]{1,0:T(1,128)} %param.22) | copy-start | bytes 52
  7.2 17.7 %copy-start.41 = (s32[1,512,3]{1,0,2:T(1,128)S(1)}, s32[1,512,3]{1,0,2:T(1,128)}, u32[]{:S(2)}) copy-start(s32[1,512,3]{1,0,2:T(1,128)} %param.24) | copy-start | bytes 18436
  7.2 19.5 %copy-start.34 = (f32[1,4,512]{2,1,0:T(4,128)S(1)}, f32[1,4,512]{2,1,0:T(4,128)}, u32[]{:S(2)}) copy-start(f32[1,4,512]{2,1,0:T(4,128)} %param.25) | copy-start | bytes 24580
  7.2 79.1 %all-gather.2.cloned.1.call-start = ((), (), s32[]{:S(2)}) async-start(), calls=%async_computation.1 | async-start | bytes 8912896 | tf_op jit(solution)/shard_map/all_gather | solution.py:61
  9.2 359.5 %reduce-scatter.2.cloned.1.call-start = ((), (), s32[]{:S(2)}) async-start(), calls=%async_computation.2 | async-start | bytes 4456448 | tf_op jit(solution)/shard_map/reduce_scatter | solution.py:119
  10.1 86.8 %collective-permute-start.5 = (f32[1,128,128]{2,1,0:T(8,128)S(1)}, f32[1,128,128]{2,1,0:T(8,128)S(1)}, u32[]{:S(2)}, u32[]{:S(2)}) collective-permute-start(f32[1,128,128]{2,1,0:T(8,128)S(1)} %get-tuple-element.66), channel_id=1, source_target_pairs={{0,1},{1,2},{2,3},{3,4},{4,5},{5,6},{6,7},{8,9},{9,10},{10,11},{11... | collective-permute-start | bytes 196616 | tf_op jit(solution)/shard_map/ppermute | solution.py:16
  14.0 82.9 %collective-permute-start.4 = (f32[1,128,128]{2,1,0:T(8,128)S(1)}, f32[1,128,128]{2,1,0:T(8,128)S(1)}, u32[]{:S(2)}, u32[]{:S(2)}) collective-permute-start(f32[1,128,128]{2,1,0:T(8,128)S(1)} %get-tuple-element.67), channel_id=1, source_target_pairs={{1,0},{2,1},{3,2},{4,3},{5,4},{6,5},{7,6},{9,8},{10,9},{11,10},{12... | collective-permute-start | bytes 196616 | tf_op jit(solution)/shard_map/ppermute | solution.py:17
  87.4 8.0 %copy-start.25 = (f32[16,128,128]{2,1,0:T(8,128)S(1)}, f32[16,128,128]{2,1,0:T(8,128)}, u32[]{:S(2)}) copy-start(f32[16,128,128]{2,1,0:T(8,128)} %slice_bitcast_fusion) | copy-start | bytes 3145732
  87.5 9.5 %collective-permute-start = (f32[1,128,128]{2,1,0:T(8,128)S(1)}, f32[1,128,128]{2,1,0:T(8,128)S(1)}, u32[]{:S(2)}, u32[]{:S(2)}) collective-permute-start(f32[1,128,128]{2,1,0:T(8,128)S(1)} %get-tuple-element.64), channel_id=1, source_target_pairs={{1,0},{2,1},{3,2},{4,3},{5,4},{6,5},{7,6},{9,8},{10,9},{11,10},{12... | collective-permute-start | bytes 196616 | tf_op jit(solution)/shard_map/ppermute | solution.py:17
  88.9 8.1 %collective-permute-start.1 = (f32[1,128,128]{2,1,0:T(8,128)S(1)}, f32[1,128,128]{2,1,0:T(8,128)S(1)}, u32[]{:S(2)}, u32[]{:S(2)}) collective-permute-start(f32[1,128,128]{2,1,0:T(8,128)S(1)} %get-tuple-element.65), channel_id=1, source_target_pairs={{0,1},{1,2},{2,3},{3,4},{4,5},{5,6},{6,7},{8,9},{9,10},{10,11},{11... | collective-permute-start | bytes 196616 | tf_op jit(solution)/shard_map/ppermute | solution.py:16
  96.9 13.2 %copy-start.2 = (f32[16,129,128]{2,1,0:T(8,128)}, f32[16,129,128]{2,1,0:T(8,128)S(1)}, u32[]{:S(2)}) copy-start(f32[16,129,128]{2,1,0:T(8,128)S(1)} %get-tuple-element.60) | copy-start | bytes 3170308
  103.3 6.8 %copy-start.9 = (f32[262144]{0:T(1024)}, f32[262144]{0:T(1024)S(1)}, u32[]{:S(2)}) copy-start(f32[262144]{0:T(1024)S(1)} %fusion.52) | copy-start | bytes 3145732
  103.3 15.8 %collective-permute-start.7 = (f32[1,128,128]{2,1,0:T(8,128)S(1)}, f32[1,128,128]{2,1,0:T(8,128)S(1)}, u32[]{:S(2)}, u32[]{:S(2)}) collective-permute-start(f32[1,128,128]{2,1,0:T(8,128)S(1)} %get-tuple-element.78), channel_id=1, source_target_pairs={{0,1},{1,2},{2,3},{3,4},{4,5},{5,6},{6,7},{8,9},{9,10},{10,11},{11... | collective-permute-start | bytes 196616 | tf_op jit(solution)/shard_map/ppermute | solution.py:16
  106.8 12.3 %collective-permute-start.6 = (f32[1,128,128]{2,1,0:T(8,128)S(1)}, f32[1,128,128]{2,1,0:T(8,128)S(1)}, u32[]{:S(2)}, u32[]{:S(2)}) collective-permute-start(f32[1,128,128]{2,1,0:T(8,128)S(1)} %get-tuple-element.79), channel_id=1, source_target_pairs={{1,0},{2,1},{3,2},{4,3},{5,4},{6,5},{7,6},{9,8},{10,9},{11,10},{12... | collective-permute-start | bytes 196616 | tf_op jit(solution)/shard_map/ppermute | solution.py:17
  126.9 7.7 %copy-start.12 = (f32[262144]{0:T(1024)}, f32[262144]{0:T(1024)S(1)}, u32[]{:S(2)}) copy-start(f32[262144]{0:T(1024)S(1)} %fusion.53) | copy-start | bytes 3145732
  127.0 16.8 %collective-permute-start.9 = (f32[1,128,128]{2,1,0:T(8,128)S(1)}, f32[1,128,128]{2,1,0:T(8,128)S(1)}, u32[]{:S(2)}, u32[]{:S(2)}) collective-permute-start(f32[1,128,128]{2,1,0:T(8,128)S(1)} %get-tuple-element.76), channel_id=1, source_target_pairs={{0,1},{1,2},{2,3},{3,4},{4,5},{5,6},{6,7},{8,9},{9,10},{10,11},{11... | collective-permute-start | bytes 196616 | tf_op jit(solution)/shard_map/ppermute | solution.py:16
  131.3 12.4 %collective-permute-start.8 = (f32[1,128,128]{2,1,0:T(8,128)S(1)}, f32[1,128,128]{2,1,0:T(8,128)S(1)}, u32[]{:S(2)}, u32[]{:S(2)}) collective-permute-start(f32[1,128,128]{2,1,0:T(8,128)S(1)} %get-tuple-element.77), channel_id=1, source_target_pairs={{1,0},{2,1},{3,2},{4,3},{5,4},{6,5},{7,6},{9,8},{10,9},{11,10},{12... | collective-permute-start | bytes 196616 | tf_op jit(solution)/shard_map/ppermute | solution.py:17
  151.6 7.9 %copy-start.15 = (f32[262144]{0:T(1024)}, f32[262144]{0:T(1024)S(1)}, u32[]{:S(2)}) copy-start(f32[262144]{0:T(1024)S(1)} %fusion.54) | copy-start | bytes 3145732
  151.6 17.0 %collective-permute-start.11 = (f32[1,128,128]{2,1,0:T(8,128)S(1)}, f32[1,128,128]{2,1,0:T(8,128)S(1)}, u32[]{:S(2)}, u32[]{:S(2)}) collective-permute-start(f32[1,128,128]{2,1,0:T(8,128)S(1)} %get-tuple-element.74), channel_id=1, source_target_pairs={{0,1},{1,2},{2,3},{3,4},{4,5},{5,6},{6,7},{8,9},{9,10},{10,11},{11... | collective-permute-start | bytes 196616 | tf_op jit(solution)/shard_map/ppermute | solution.py:16
  156.0 12.6 %collective-permute-start.10 = (f32[1,128,128]{2,1,0:T(8,128)S(1)}, f32[1,128,128]{2,1,0:T(8,128)S(1)}, u32[]{:S(2)}, u32[]{:S(2)}) collective-permute-start(f32[1,128,128]{2,1,0:T(8,128)S(1)} %get-tuple-element.75), channel_id=1, source_target_pairs={{1,0},{2,1},{3,2},{4,3},{5,4},{6,5},{7,6},{9,8},{10,9},{11,10},{12... | collective-permute-start | bytes 196616 | tf_op jit(solution)/shard_map/ppermute | solution.py:17
  171.1 5.4 %copy-start.5 = (f32[16,129,128]{2,1,0:T(8,128)S(1)}, f32[16,129,128]{2,1,0:T(8,128)}, u32[]{:S(2)}) copy-start(f32[16,129,128]{2,1,0:T(8,128)} %copy-done.2) | copy-start | bytes 3170308
  179.8 15.0 %copy-start.36 = (f32[1,1,512]{2,1,0:T(1,128)S(1)}, f32[1,1,512]{2,1,0:T(1,128)}, u32[]{:S(2)}) copy-start(f32[1,1,512]{2,1,0:T(1,128)} %get-tuple-element.84) | copy-start | bytes 6148
  179.8 15.0 %copy-start.37 = (f32[1,1,512]{2,1,0:T(1,128)S(1)}, f32[1,1,512]{2,1,0:T(1,128)}, u32[]{:S(2)}) copy-start(f32[1,1,512]{2,1,0:T(1,128)} %get-tuple-element.85) | copy-start | bytes 6148
  179.8 15.0 %copy-start.38 = (f32[512]{0:T(512)S(1)}, f32[512]{0:T(512)}, u32[]{:S(2)}) copy-start(f32[512]{0:T(512)} %gather_fusion.3) | copy-start | bytes 6148
  179.8 15.0 %copy-start.39 = (f32[512]{0:T(512)S(1)}, f32[512]{0:T(512)}, u32[]{:S(2)}) copy-start(f32[512]{0:T(512)} %gather_fusion.2) | copy-start | bytes 6148
  179.8 15.0 %copy-start.40 = (f32[512]{0:T(512)S(1)}, f32[512]{0:T(512)}, u32[]{:S(2)}) copy-start(f32[512]{0:T(512)} %gather_fusion.1) | copy-start | bytes 6148
  179.8 15.0 %copy-start.43 = (pred[512]{0:T(512)(128)(4,1)S(1)}, pred[512]{0:T(512)(128)(4,1)}, u32[]{:S(2)}) copy-start(pred[512]{0:T(512)(128)(4,1)} %and_reduce_fusion) | copy-start | bytes 1540
  188.4 6.9 %collective-permute-start.3 = (f32[1,128,128]{2,1,0:T(8,128)S(1)}, f32[1,128,128]{2,1,0:T(8,128)S(1)}, u32[]{:S(2)}, u32[]{:S(2)}) collective-permute-start(f32[1,128,128]{2,1,0:T(8,128)S(1)} %get-tuple-element.80), channel_id=1, source_target_pairs={{0,1},{1,2},{2,3},{3,4},{4,5},{5,6},{6,7},{8,9},{9,10},{10,11},{11... | collective-permute-start | bytes 196616 | tf_op jit(solution)/shard_map/ppermute | solution.py:16
  193.5 6.9 %collective-permute-start.2 = (f32[1,128,128]{2,1,0:T(8,128)S(1)}, f32[1,128,128]{2,1,0:T(8,128)S(1)}, u32[]{:S(2)}, u32[]{:S(2)}) collective-permute-start(f32[1,128,128]{2,1,0:T(8,128)S(1)} %get-tuple-element.81), channel_id=1, source_target_pairs={{1,0},{2,1},{3,2},{4,3},{5,4},{6,5},{7,6},{9,8},{10,9},{11,10},{12... | collective-permute-start | bytes 196616 | tf_op jit(solution)/shard_map/ppermute | solution.py:17
  194.8 7.3 %copy-start.26 = (f32[16,129,128]{2,1,0:T(8,128)S(1)}, f32[16,129,128]{2,1,0:T(8,128)}, u32[]{:S(2)}) copy-start(f32[16,129,128]{2,1,0:T(8,128)} %subtract_multiply_fusion.7) | copy-start | bytes 3170308
  194.9 7.3 %copy-start.31 = (f32[16,128,129]{2,1,0:T(8,128)S(1)}, f32[16,128,129]{2,1,0:T(8,128)}, u32[]{:S(2)}) copy-start(f32[16,128,129]{2,1,0:T(8,128)} %fusion.3) | copy-start | bytes 3170308
  212.8 6.8 %copy-start.6 = (f32[16,129,128]{2,1,0:T(8,128)S(1)}, f32[16,129,128]{2,1,0:T(8,128)}, u32[]{:S(2)}) copy-start(f32[16,129,128]{2,1,0:T(8,128)} %copy-done.2) | copy-start | bytes 3170308
  213.5 6.7 %collective-permute-start.13 = (f32[1,128,128]{2,1,0:T(8,128)S(1)}, f32[1,128,128]{2,1,0:T(8,128)S(1)}, u32[]{:S(2)}, u32[]{:S(2)}) collective-permute-start(f32[1,128,128]{2,1,0:T(8,128)S(1)} %get-tuple-element.72), channel_id=1, source_target_pairs={{0,1},{1,2},{2,3},{3,4},{4,5},{5,6},{6,7},{8,9},{9,10},{10,11},{11... | collective-permute-start | bytes 196616 | tf_op jit(solution)/shard_map/ppermute | solution.py:16
  218.3 6.2 %collective-permute-start.12 = (f32[1,128,128]{2,1,0:T(8,128)S(1)}, f32[1,128,128]{2,1,0:T(8,128)S(1)}, u32[]{:S(2)}, u32[]{:S(2)}) collective-permute-start(f32[1,128,128]{2,1,0:T(8,128)S(1)} %get-tuple-element.73), channel_id=1, source_target_pairs={{1,0},{2,1},{3,2},{4,3},{5,4},{6,5},{7,6},{9,8},{10,9},{11,10},{12... | collective-permute-start | bytes 196616 | tf_op jit(solution)/shard_map/ppermute | solution.py:17
  219.8 4.9 %copy-start.18 = (f32[262144]{0:T(1024)S(1)}, f32[262144]{0:T(1024)}, u32[]{:S(2)}) copy-start(f32[262144]{0:T(1024)} %scatter_fusion) | copy-start | bytes 3145732
  219.8 4.9 %copy-start.32 = (f32[1,2,16,128,128]{4,3,2,1,0:T(8,128)S(1)}, f32[1,2,16,128,128]{4,3,2,1,0:T(8,128)}, u32[]{:S(2)}) copy-start(f32[1,2,16,128,128]{4,3,2,1,0:T(8,128)} %param.21) | copy-start | bytes 6291460
  233.7 5.0 %copy-start.7 = (f32[16,129,128]{2,1,0:T(8,128)S(1)}, f32[16,129,128]{2,1,0:T(8,128)}, u32[]{:S(2)}) copy-start(f32[16,129,128]{2,1,0:T(8,128)} %copy-done.2) | copy-start | bytes 3170308
  234.3 4.7 %collective-permute-start.15 = (f32[1,128,128]{2,1,0:T(8,128)S(1)}, f32[1,128,128]{2,1,0:T(8,128)S(1)}, u32[]{:S(2)}, u32[]{:S(2)}) collective-permute-start(f32[1,128,128]{2,1,0:T(8,128)S(1)} %get-tuple-element.70), channel_id=1, source_target_pairs={{0,1},{1,2},{2,3},{3,4},{4,5},{5,6},{6,7},{8,9},{9,10},{10,11},{11... | collective-permute-start | bytes 196616 | tf_op jit(solution)/shard_map/ppermute | solution.py:16
  237.2 6.2 %collective-permute-start.14 = (f32[1,128,128]{2,1,0:T(8,128)S(1)}, f32[1,128,128]{2,1,0:T(8,128)S(1)}, u32[]{:S(2)}, u32[]{:S(2)}) collective-permute-start(f32[1,128,128]{2,1,0:T(8,128)S(1)} %get-tuple-element.71), channel_id=1, source_target_pairs={{1,0},{2,1},{3,2},{4,3},{5,4},{6,5},{7,6},{9,8},{10,9},{11,10},{12... | collective-permute-start | bytes 196616 | tf_op jit(solution)/shard_map/ppermute | solution.py:17
  252.5 6.8 %copy-start.8 = (f32[16,129,128]{2,1,0:T(8,128)S(1)}, f32[16,129,128]{2,1,0:T(8,128)}, u32[]{:S(2)}) copy-start(f32[16,129,128]{2,1,0:T(8,128)} %copy-done.2) | copy-start | bytes 3170308
  253.2 6.7 %collective-permute-start.17 = (f32[1,128,128]{2,1,0:T(8,128)S(1)}, f32[1,128,128]{2,1,0:T(8,128)S(1)}, u32[]{:S(2)}, u32[]{:S(2)}) collective-permute-start(f32[1,128,128]{2,1,0:T(8,128)S(1)} %get-tuple-element.68), channel_id=1, source_target_pairs={{0,1},{1,2},{2,3},{3,4},{4,5},{5,6},{6,7},{8,9},{9,10},{10,11},{11... | collective-permute-start | bytes 196616 | tf_op jit(solution)/shard_map/ppermute | solution.py:16
  258.0 6.2 %collective-permute-start.16 = (f32[1,128,128]{2,1,0:T(8,128)S(1)}, f32[1,128,128]{2,1,0:T(8,128)S(1)}, u32[]{:S(2)}, u32[]{:S(2)}) collective-permute-start(f32[1,128,128]{2,1,0:T(8,128)S(1)} %get-tuple-element.69), channel_id=1, source_target_pairs={{1,0},{2,1},{3,2},{4,3},{5,4},{6,5},{7,6},{9,8},{10,9},{11,10},{12... | collective-permute-start | bytes 196616 | tf_op jit(solution)/shard_map/ppermute | solution.py:17
  259.4 4.9 %copy-start.22 = (f32[262144]{0:T(1024)S(1)}, f32[262144]{0:T(1024)}, u32[]{:S(2)}) copy-start(f32[262144]{0:T(1024)} %scatter_fusion.1) | copy-start | bytes 3145732
  259.5 4.9 %copy-start.23 = (f32[262144]{0:T(1024)S(1)}, f32[262144]{0:T(1024)}, u32[]{:S(2)}) copy-start(f32[262144]{0:T(1024)} %scatter_fusion.2) | copy-start | bytes 3145732
  265.9 5.3 %copy-start.20 = (f32[262144]{0:T(1024)S(1)}, f32[262144]{0:T(1024)}, u32[]{:S(2)}) copy-start(f32[262144]{0:T(1024)} %scatter_fusion) | copy-start | bytes 3145732
  293.0 75.6 %copy-start.1 = (s32[16,2]{0,1:T(2,128)S(1)}, s32[16,2]{0,1:T(2,128)}, u32[]{:S(2)}) copy-start(s32[16,2]{0,1:T(2,128)} %param.19) | copy-start | bytes 388
  (16 other events, 37.7 us)
Sparse Core Ops, SparseCore 0:
  11.1 75.2 all-gather.1
  291.9 76.6 reduce-scatter.1
where the time goes:
time: 378 us; the launch traced here: 375 us
  waiting for transfers between devices  148 us (39%)
  other arithmetic  93.7 us (25%)
  local copies, waits for them, and re-layouts  59.9 us (16%)
  starting transfers between devices  50.4 us (13%)
  between operations  23.8 us (6%)
    reduce_scatter x1, waiting for transfers between devices, shards(): lax.psum_scatter(embedded, 'shot', scatter_dimension=1, tiled=True)  71.7 us
    all_gather x1, waiting for transfers between devices, shards(): gathered = lax.all_gather(stacked, 'shot', axis=2, tiled=True)  56.8 us
    ppermute x9, starting transfers between devices, with_halo(): before = lax.ppermute(last, axis, up)  38.2 us
    gather x4, local copies, waits for them, and re-layouts, shards(): sampled = following.reshape(-1)[receiver_flat]  30.3 us
    scatter-add x8, other arithmetic, add_cells(): return field.reshape(-1).at[positions].add(amounts).reshape(shape)  25.4 us
    add x4, other arithmetic, shards(): following = 2.0 * current - before + kappa_window * spread  18.3 us
    ppermute x9, waiting for transfers between devices, with_halo(): after = lax.ppermute(first, axis, down)  17.8 us
    dynamic_update_slice x1, local copies, waits for them, and re-layouts, shards(): lax.dynamic_update_slice(jnp.zeros((depth_cells, own_rows * groups, model...  13.9 us
  transfers between devices with their start and end apart: 20, of which 10 were waited for; matrix products, arithmetic and copies ran while one was open for 13% of the time, Pallas kernels for 0%

commit v1 on v0

--- a/solution.py
+++ b/solution.py
@@ -58,7 +58,10 @@
     row_anchor = anchor[0]
     col_anchor = anchor[1]
     stacked = jnp.stack([kappa, buoyancy])
-    gathered = lax.all_gather(stacked, "shot", axis=2, tiled=True)
+    size = lax.axis_size("shot")
+    blocks = jnp.stack([stacked for _ in range(size)])
+    blocks = lax.all_to_all(blocks, "shot", split_axis=0, concat_axis=0)
+    gathered = jnp.concatenate(blocks, axis=2)
     window = lax.dynamic_slice(
         gathered,
         (row_anchor * 0, row_anchor * 0, row_anchor, col_anchor),

time: 378 us -> 430 us (1.14)
  waiting for transfers between devices: 148 us -> 180 us
  starting transfers between devices: 50.4 us -> 69.1 us
    all_to_all x0 -> x1, waiting for transfers between devices: none -> 91.4 us  [shards(): blocks = lax.all_to_all(blocks, 'shot', split_axis=0, concat_axis=0)]
    all_gather x1 -> x0, waiting for transfers between devices: 56.8 us -> none  [shards(): gathered = lax.all_gather(stacked, 'shot', axis=2, tiled=True)]
    ppermute x9, waiting for transfers between devices: 17.8 us -> 0.44 us  [with_halo(): after = lax.ppermute(first, axis, down)]
    ppermute x9, starting transfers between devices: 38.2 us -> 49.2 us  [with_halo(): before = lax.ppermute(last, axis, up)]
    reduce_scatter x1, waiting for transfers between devices: 71.7 us -> 81.1 us  [shards(): lax.psum_scatter(embedded, 'shot', scatter_dimension=1, tiled=True)]
    all_to_all x0 -> x1, starting transfers between devices: none -> 8.13 us  [shards(): blocks = lax.all_to_all(blocks, 'shot', split_axis=0, concat_axis=0)]
    ppermute x9, waiting for transfers between devices: 1.45 us -> 6.82 us  [with_halo(): before = lax.ppermute(last, axis, up)]
    all_to_all x0 -> x1, local copies, waits for them, and re-layouts: none -> 4.37 us  [shards(): blocks = lax.all_to_all(blocks, 'shot', split_axis=0, concat_axis=0)]
  transfers between devices with their start and end apart: 20 -> 20, of which waited for: 10 -> 10; matrix products, arithmetic and copies ran while one was open for 13% -> 11% of each run, Pallas kernels for 0% -> 0%
where the time goes in v1:
time: 430 us; the launch traced here: 427 us
  waiting for transfers between devices  180 us (42%)
  other arithmetic  91.4 us (21%)
  starting transfers between devices  69.1 us (16%)
  local copies, waits for them, and re-layouts  63.3 us (15%)
  between operations  23.8 us (6%)
    all_to_all x1, waiting for transfers between devices, shards(): blocks = lax.all_to_all(blocks, 'shot', split_axis=0, concat_axis=0)  91.4 us
    reduce_scatter x1, waiting for transfers between devices, shards(): lax.psum_scatter(embedded, 'shot', scatter_dimension=1, tiled=True)  81.1 us
    ppermute x9, starting transfers between devices, with_halo(): before = lax.ppermute(last, axis, up)  49.2 us
    gather x4, local copies, waits for them, and re-layouts, shards(): sampled = following.reshape(-1)[receiver_flat]  30.4 us
    scatter-add x8, other arithmetic, add_cells(): return field.reshape(-1).at[positions].add(amounts).reshape(shape)  25.6 us
    add x4, other arithmetic, shards(): following = 2.0 * current - before + kappa_window * spread  16.3 us
    dynamic_update_slice x1, local copies, waits for them, and re-layouts, shards(): lax.dynamic_update_slice(jnp.zeros((depth_cells, own_rows * groups, model...  13.9 us
    ppermute x9, starting transfers between devices, with_halo(): after = lax.ppermute(first, axis, down)  11.8 us
  transfers between devices with their start and end apart: 20, of which 10 were waited for; matrix products, arithmetic and copies ran while one was open for 11% of the time, Pallas kernels for 0%

profile of v1, /device:TPU:0, one launch (start us, length us, event | category | flops | bytes accessed | tf_op | source)
XLA Modules:
  0.0 427.3 jit_solution(1192916603539917368)
XLA Ops:
  8.3 4.4 %stack.15 = f32[16,2,16,16,256]{4,3,2,1,0:T(8,128)} broadcast(f32[2,16,16,256]{3,2,1,0:T(8,128)S(1)} %pad_maximum_fusion), dimensions={1,2,3,4} | broadcast | bytes 8912896 | tf_op jit(solution)/shard_map/stack | solution.py:62
  12.6 8.1 %all-to-all-start = ((f32[16,2,16,16,256]{4,3,2,1,0:T(8,128)}), f32[16,2,16,16,256]{4,3,2,1,0:T(8,128)}, u32[]{:S(2)}, u32[]{:S(2)}) async-start(f32[16,2,16,16,256]{4,3,2,1,0:T(8,128)} %stack.15), calls=%async_computation | async-start | bytes 16777216 | tf_op jit(solution)/shard_map/all_to_all | solution.py:63
  22.1 4.5 %collective-permute-start.5 = (f32[1,128,128]{2,1,0:T(8,128)S(1)}, f32[1,128,128]{2,1,0:T(8,128)S(1)}, u32[]{:S(2)}, u32[]{:S(2)}) collective-permute-start(f32[1,128,128]{2,1,0:T(8,128)S(1)} %get-tuple-element.66), channel_id=1, source_target_pairs={{0,1},{1,2},{2,3},{3,4},{4,5},{5,6},{6,7},{8,9},{9,10},{10,11},{11... | collective-permute-start | bytes 196616 | tf_op jit(solution)/shard_map/ppermute | solution.py:16
  39.9 91.4 %all-to-all-done = f32[16,2,16,16,256]{4,3,2,1,0:T(8,128)} async-done(((f32[16,2,16,16,256]{4,3,2,1,0:T(8,128)}), f32[16,2,16,16,256]{4,3,2,1,0:T(8,128)}, u32[]{:S(2)}, u32[]{:S(2)}) %all-to-all-start) | async-done | bytes 8388640 | tf_op jit(solution)/shard_map/all_to_all | solution.py:63
  131.2 4.4 %copy.12 = f32[16,2,16,16,256]{4,3,0,2,1:T(8,128)S(1)} copy(f32[16,2,16,16,256]{4,3,2,1,0:T(8,128)} %all-to-all-done) | data formatting | bytes 16777216 | tf_op jit(solution)/shard_map/all_to_all | solution.py:63
  137.5 6.1 %collective-permute-start.1 = (f32[1,128,128]{2,1,0:T(8,128)S(1)}, f32[1,128,128]{2,1,0:T(8,128)S(1)}, u32[]{:S(2)}, u32[]{:S(2)}) collective-permute-start(f32[1,128,128]{2,1,0:T(8,128)S(1)} %get-tuple-element.65), channel_id=1, source_target_pairs={{0,1},{1,2},{2,3},{3,4},{4,5},{5,6},{6,7},{8,9},{9,10},{10,11},{11... | collective-permute-start | bytes 196616 | tf_op jit(solution)/shard_map/ppermute | solution.py:16
  147.1 1.9 fusion.47
  151.2 5.4 %collective-permute-start.7 = (f32[1,128,128]{2,1,0:T(8,128)S(1)}, f32[1,128,128]{2,1,0:T(8,128)S(1)}, u32[]{:S(2)}, u32[]{:S(2)}) collective-permute-start(f32[1,128,128]{2,1,0:T(8,128)S(1)} %get-tuple-element.78), channel_id=1, source_target_pairs={{0,1},{1,2},{2,3},{3,4},{4,5},{5,6},{6,7},{8,9},{9,10},{10,11},{11... | collective-permute-start | bytes 196616 | tf_op jit(solution)/shard_map/ppermute | solution.py:16
  156.7 2.0 fusion.7
  159.8 7.9 %gather_fusion.3 = f32[512]{0:T(512)} fusion(f32[262144]{0:T(1024)} %copy-done.9, s32[1024]{0:T(1024)S(1)} %pad_clamp_fusion), kind=kCustom, calls=%fused_computation.3 | custom fusion | bytes 6144 | tf_op jit(solution)/shard_map/gather | solution.py:103
  167.8 2.0 fusion.21
  169.9 4.8 %multiply_add_fusion.3 = (f32[16,128,128]{2,1,0:T(8,128)S(1)}, f32[16,128,128]{2,1,0:T(8,128)}) fusion(f32[16,128,128]{2,1,0:T(8,128)S(1)} %bitcast.117, f32[2,16,256,256]{3,2,1,0:T(8,128)} %bitcast.149, s32[]{:T(128)S(6)} %select_n.55, s32[]{:T(128)S(6)} %select_n.56, f32[1,2,16,128,128]{4,3,2,1,0:T(8,128)} %param.20, f32[16,128,129]{2,1,0:T(8,128)} %fusion.7, ...), kind=kLoop, calls=%fused_computation.128 | loop fusion | flops 2359296 | bytes 11534344 | tf_op jit(solution)/shard_map/add | solution.py:99
  176.9 5.3 %collective-permute-start.9 = (f32[1,128,128]{2,1,0:T(8,128)S(1)}, f32[1,128,128]{2,1,0:T(8,128)S(1)}, u32[]{:S(2)}, u32[]{:S(2)}) collective-permute-start(f32[1,128,128]{2,1,0:T(8,128)S(1)} %get-tuple-element.76), channel_id=1, source_target_pairs={{0,1},{1,2},{2,3},{3,4},{4,5},{5,6},{6,7},{8,9},{9,10},{10,11},{11... | collective-permute-start | bytes 196616 | tf_op jit(solution)/shard_map/ppermute | solution.py:16
  182.2 2.0 fusion.9
  185.4 7.8 %gather_fusion.2 = f32[512]{0:T(512)} fusion(f32[262144]{0:T(1024)} %copy-done.12, s32[1024]{0:T(1024)S(1)} %pad_clamp_fusion), kind=kCustom, calls=%fused_computation.2 | custom fusion | bytes 6144 | tf_op jit(solution)/shard_map/gather | solution.py:103
  193.2 2.0 fusion.22
  195.7 4.5 %multiply_add_fusion.2 = (f32[16,128,128]{2,1,0:T(8,128)S(1)}, f32[16,128,128]{2,1,0:T(8,128)}) fusion(f32[16,128,128]{2,1,0:T(8,128)S(1)} %bitcast.118, f32[16,128,128]{2,1,0:T(8,128)S(1)} %bitcast.123, f32[2,16,256,256]{3,2,1,0:T(8,128)} %bitcast.150, s32[]{:T(128)S(6)} %select_n.55, s32[]{:T(128)S(6)} %select_n.56, f32[16,128,129]{2,1,0:T(8,128)} %fusion.9, ...), kind=kLoop, calls=%fused_computation.127 | loop fusion | flops 2359296 | bytes 11534344 | tf_op jit(solution)/shard_map/add | solution.py:99
  202.4 5.4 %collective-permute-start.11 = (f32[1,128,128]{2,1,0:T(8,128)S(1)}, f32[1,128,128]{2,1,0:T(8,128)S(1)}, u32[]{:S(2)}, u32[]{:S(2)}) collective-permute-start(f32[1,128,128]{2,1,0:T(8,128)S(1)} %get-tuple-element.74), channel_id=1, source_target_pairs={{0,1},{1,2},{2,3},{3,4},{4,5},{5,6},{6,7},{8,9},{9,10},{10,11},{11... | collective-permute-start | bytes 196616 | tf_op jit(solution)/shard_map/ppermute | solution.py:16
  207.8 2.0 fusion.11
  210.9 7.9 %gather_fusion.1 = f32[512]{0:T(512)} fusion(f32[262144]{0:T(1024)} %copy-done.15, s32[1024]{0:T(1024)S(1)} %pad_clamp_fusion), kind=kCustom, calls=%fused_computation.1 | custom fusion | bytes 6144 | tf_op jit(solution)/shard_map/gather | solution.py:103
  218.9 2.0 fusion.23
  221.4 5.1 %multiply_add_fusion.1 = (f32[16,128,128]{2,1,0:T(8,128)}, f32[16,128,128]{2,1,0:T(8,128)}, f32[16,128,128]{2,1,0:T(8,128)S(1)}) fusion(f32[16,128,128]{2,1,0:T(8,128)S(1)} %bitcast.124, f32[16,128,128]{2,1,0:T(8,128)S(1)} %bitcast.129, f32[2,16,256,256]{3,2,1,0:T(8,128)} %bitcast.151, s32[]{:T(128)S(6)} %select_n.55, s32[]{:T(128)S(6)} %select_n.56, ...), kind=kLoop, calls=%fused_computation.126 | loop fusion | flops 2621440 | bytes 13631496 | tf_op jit(solution)/shard_map/add | solution.py:99
  227.8 2.0 fusion.3
  229.8 2.2 fusion.55
  232.0 6.7 %gather_fusion = f32[512]{0:T(512)S(1)} fusion(f32[262144]{0:T(1024)} %fusion.55, s32[1024]{0:T(1024)S(1)} %pad_clamp_fusion), kind=kCustom, calls=%fused_computation | custom fusion | bytes 6144 | tf_op jit(solution)/shard_map/gather | solution.py:103
  240.0 5.1 %collective-permute-start.3 = (f32[1,128,128]{2,1,0:T(8,128)S(1)}, f32[1,128,128]{2,1,0:T(8,128)S(1)}, u32[]{:S(2)}, u32[]{:S(2)}) collective-permute-start(f32[1,128,128]{2,1,0:T(8,128)S(1)} %get-tuple-element.80), channel_id=1, source_target_pairs={{0,1},{1,2},{2,3},{3,4},{4,5},{5,6},{6,7},{8,9},{9,10},{10,11},{11... | collective-permute-start | bytes 196616 | tf_op jit(solution)/shard_map/ppermute | solution.py:16
  245.5 1.6 collective-permute-done.3
  247.1 1.9 fusion.19
  249.0 3.0 fusion.45
  251.9 5.2 %scatter_fusion = f32[262144]{0:T(1024)} fusion(f32[262144]{0:T(1024)} %bitcast.131, s32[512]{0:T(512)S(1)} %bitcast.161, f32[512]{0:T(512)S(1)} %get-tuple-element.91), kind=kCustom, calls=%fused_computation.4 | custom fusion | flops 512 | bytes 8192 | tf_op jit(solution)/shard_map/scatter-add | solution.py:37
  257.1 2.3 fusion.50
  261.4 5.4 %collective-permute-start.13 = (f32[1,128,128]{2,1,0:T(8,128)S(1)}, f32[1,128,128]{2,1,0:T(8,128)S(1)}, u32[]{:S(2)}, u32[]{:S(2)}) collective-permute-start(f32[1,128,128]{2,1,0:T(8,128)S(1)} %get-tuple-element.72), channel_id=1, source_target_pairs={{0,1},{1,2},{2,3},{3,4},{4,5},{5,6},{6,7},{8,9},{9,10},{10,11},{11... | collective-permute-start | bytes 196616 | tf_op jit(solution)/shard_map/ppermute | solution.py:16
  267.2 1.6 collective-permute-done.13
  270.4 5.2 %scatter_fusion.1 = f32[262144]{0:T(1024)} fusion(f32[262144]{0:T(1024)} %bitcast.136, s32[512]{0:T(512)S(1)} %bitcast.162, f32[512]{0:T(512)S(1)} %get-tuple-element.90), kind=kCustom, calls=%fused_computation.5 | custom fusion | flops 512 | bytes 8192 | tf_op jit(solution)/shard_map/scatter-add | solution.py:37
  275.6 2.3 fusion.49
  279.9 6.0 %collective-permute-start.15 = (f32[1,128,128]{2,1,0:T(8,128)S(1)}, f32[1,128,128]{2,1,0:T(8,128)S(1)}, u32[]{:S(2)}, u32[]{:S(2)}) collective-permute-start(f32[1,128,128]{2,1,0:T(8,128)S(1)} %get-tuple-element.70), channel_id=1, source_target_pairs={{0,1},{1,2},{2,3},{3,4},{4,5},{5,6},{6,7},{8,9},{9,10},{10,11},{11... | collective-permute-start | bytes 196616 | tf_op jit(solution)/shard_map/ppermute | solution.py:16
  287.8 1.5 fusion.31
  289.3 5.2 %scatter_fusion.2 = f32[262144]{0:T(1024)} fusion(f32[262144]{0:T(1024)} %bitcast.141, s32[512]{0:T(512)S(1)} %bitcast.163, f32[512]{0:T(512)S(1)} %get-tuple-element.89), kind=kCustom, calls=%fused_computation.6 | custom fusion | flops 512 | bytes 8192 | tf_op jit(solution)/shard_map/scatter-add | solution.py:37
  294.5 2.3 fusion.48
  298.8 5.8 %collective-permute-start.17 = (f32[1,128,128]{2,1,0:T(8,128)S(1)}, f32[1,128,128]{2,1,0:T(8,128)S(1)}, u32[]{:S(2)}, u32[]{:S(2)}) collective-permute-start(f32[1,128,128]{2,1,0:T(8,128)S(1)} %get-tuple-element.68), channel_id=1, source_target_pairs={{0,1},{1,2},{2,3},{3,4},{4,5},{5,6},{6,7},{8,9},{9,10},{10,11},{11... | collective-permute-start | bytes 196616 | tf_op jit(solution)/shard_map/ppermute | solution.py:16
  304.8 1.6 collective-permute-done.17
  306.6 1.6 fusion.28
  308.2 5.3 %scatter_fusion.3 = f32[262144]{0:T(1024)} fusion(f32[262144]{0:T(1024)} %bitcast.155, s32[512]{0:T(512)S(1)} %bitcast.164, f32[512]{0:T(512)S(1)} %get-tuple-element.88), kind=kCustom, calls=%fused_computation.7 | custom fusion | flops 512 | bytes 8192 | tf_op jit(solution)/shard_map/scatter-add | solution.py:37
  313.5 4.4 %multiply_add_fusion = f32[16,128,128]{2,1,0:T(8,128)} fusion(f32[16,128,128]{2,1,0:T(8,128)} %bitcast.156, f32[16,128,128]{2,1,0:T(8,128)} %get-tuple-element.58, f32[16,128,128]{2,1,0:T(8,128)S(1)} %bitcast.144, f32[16,128,128]{2,1,0:T(8,128)} %get-tuple-element.56, f32[16,128,128]{2,1,0:T(8,128)S(1)} %bitcast.140, f32[16,128,128]{2,1,0:T(8,128)} %get-tuple-element.54, ...), kind=kLoop, calls=%fused_computation.125 | loop fusion | flops 1835008 | bytes 9437184 | tf_op jit(solution)/shard_map/add | solution.py:114
  317.8 2.4 broadcast_in_dim.15
  320.3 13.9 %dynamic_update_slice.3 = f32[16,256,256]{2,1,0:T(8,128)} dynamic-update-slice(f32[16,256,256]{2,1,0:T(8,128)} %broadcast_in_dim.15, f32[16,128,128]{2,1,0:T(8,128)S(1)} %copy-done.36, s32[]{:T(128)} %constant.95.clone.1, s32[]{:T(128)S(6)} %select_n.55, s32[]{:T(128)S(6)} %select_n.56) | dynamic-update-slice | bytes 2097156 | tf_op jit(solution)/shard_map/dynamic_update_slice | solution.py:117
  335.7 3.7 maximum_bitcast_fusion
  339.4 81.1 %reduce-scatter.2.cloned.1.call-done = f32[16,16,256]{2,1,0:T(8,128)} async-done(((f32[16,256,256]{2,1,0:T(8,128)}), f32[16,16,256]{2,1,0:T(8,128)}) %reduce-scatter.2.cloned.1.call-update) | async-done | bytes 262160 | tf_op jit(solution)/shard_map/reduce_scatter | solution.py:122
  (162 shorter events, 37.4 us)
Async XLA Ops:
  7.2 19.5 %copy-start = (s32[16,2]{0,1:T(2,128)S(1)}, s32[16,2]{0,1:T(2,128)}, u32[]{:S(2)}) copy-start(s32[16,2]{0,1:T(2,128)} %param.19) | copy-start | bytes 388
  12.6 8.2 %copy-start.32 = (f32[1,2,16,128,128]{4,3,2,1,0:T(8,128)S(1)}, f32[1,2,16,128,128]{4,3,2,1,0:T(8,128)}, u32[]{:S(2)}) copy-start(f32[1,2,16,128,128]{4,3,2,1,0:T(8,128)} %param.20) | copy-start | bytes 6291460
  12.6 17.3 %copy-start.45 = (s32[1,3]{1,0:T(1,128)S(1)}, s32[1,3]{1,0:T(1,128)}, u32[]{:S(2)}) copy-start(s32[1,3]{1,0:T(1,128)} %param.23) | copy-start | bytes 40
  12.6 20.4 %copy-start.38 = (f32[1,4]{1,0:T(1,128)S(1)}, f32[1,4]{1,0:T(1,128)}, u32[]{:S(2)}) copy-start(f32[1,4]{1,0:T(1,128)} %param.22) | copy-start | bytes 52
  12.6 23.7 %copy-start.44 = (s32[1,512,3]{1,0,2:T(1,128)S(1)}, s32[1,512,3]{1,0,2:T(1,128)}, u32[]{:S(2)}) copy-start(s32[1,512,3]{1,0,2:T(1,128)} %param.24) | copy-start | bytes 18436
  12.6 25.6 %copy-start.37 = (f32[1,4,512]{2,1,0:T(4,128)S(1)}, f32[1,4,512]{2,1,0:T(4,128)}, u32[]{:S(2)}) copy-start(f32[1,4,512]{2,1,0:T(4,128)} %param.25) | copy-start | bytes 24580
  12.6 118.6 %all-to-all-start = ((f32[16,2,16,16,256]{4,3,2,1,0:T(8,128)}), f32[16,2,16,16,256]{4,3,2,1,0:T(8,128)}, u32[]{:S(2)}, u32[]{:S(2)}) async-start(f32[16,2,16,16,256]{4,3,2,1,0:T(8,128)} %stack.15), calls=%async_computation | async-start | bytes 16777216 | tf_op jit(solution)/shard_map/all_to_all | solution.py:63
  20.8 399.7 %reduce-scatter.2.cloned.1.call-start = ((), (), s32[]{:S(2)}) async-start(), calls=%async_computation.2 | async-start | bytes 4456448 | tf_op jit(solution)/shard_map/reduce_scatter | solution.py:122
  20.8 124.3 %collective-permute-start.4 = (f32[1,128,128]{2,1,0:T(8,128)S(1)}, f32[1,128,128]{2,1,0:T(8,128)S(1)}, u32[]{:S(2)}, u32[]{:S(2)}) collective-permute-start(f32[1,128,128]{2,1,0:T(8,128)S(1)} %get-tuple-element.67), channel_id=1, source_target_pairs={{1,0},{2,1},{3,2},{4,3},{5,4},{6,5},{7,6},{9,8},{10,9},{11,10},{12... | collective-permute-start | bytes 196616 | tf_op jit(solution)/shard_map/ppermute | solution.py:17
  22.1 123.0 %collective-permute-start.5 = (f32[1,128,128]{2,1,0:T(8,128)S(1)}, f32[1,128,128]{2,1,0:T(8,128)S(1)}, u32[]{:S(2)}, u32[]{:S(2)}) collective-permute-start(f32[1,128,128]{2,1,0:T(8,128)S(1)} %get-tuple-element.66), channel_id=1, source_target_pairs={{0,1},{1,2},{2,3},{3,4},{4,5},{5,6},{6,7},{8,9},{9,10},{10,11},{11... | collective-permute-start | bytes 196616 | tf_op jit(solution)/shard_map/ppermute | solution.py:16
  135.6 10.4 %copy-start.24 = (f32[16,2,16,16,256]{4,3,0,2,1:T(8,128)}, f32[16,2,16,16,256]{4,3,0,2,1:T(8,128)S(1)}, u32[]{:S(2)}) copy-start(f32[16,2,16,16,256]{4,3,0,2,1:T(8,128)S(1)} %copy.12) | copy-start | bytes 25165828
  135.6 8.0 %copy-start.27 = (f32[16,128,128]{2,1,0:T(8,128)S(1)}, f32[16,128,128]{2,1,0:T(8,128)}, u32[]{:S(2)}) copy-start(f32[16,128,128]{2,1,0:T(8,128)} %slice_bitcast_fusion) | copy-start | bytes 3145732
  136.1 9.1 %collective-permute-start = (f32[1,128,128]{2,1,0:T(8,128)S(1)}, f32[1,128,128]{2,1,0:T(8,128)S(1)}, u32[]{:S(2)}, u32[]{:S(2)}) collective-permute-start(f32[1,128,128]{2,1,0:T(8,128)S(1)} %get-tuple-element.64), channel_id=1, source_target_pairs={{1,0},{2,1},{3,2},{4,3},{5,4},{6,5},{7,6},{9,8},{10,9},{11,10},{12... | collective-permute-start | bytes 196616 | tf_op jit(solution)/shard_map/ppermute | solution.py:17
  137.5 8.2 %collective-permute-start.1 = (f32[1,128,128]{2,1,0:T(8,128)S(1)}, f32[1,128,128]{2,1,0:T(8,128)S(1)}, u32[]{:S(2)}, u32[]{:S(2)}) collective-permute-start(f32[1,128,128]{2,1,0:T(8,128)S(1)} %get-tuple-element.65), channel_id=1, source_target_pairs={{0,1},{1,2},{2,3},{3,4},{4,5},{5,6},{6,7},{8,9},{9,10},{10,11},{11... | collective-permute-start | bytes 196616 | tf_op jit(solution)/shard_map/ppermute | solution.py:16
  145.1 13.6 %copy-start.2 = (f32[16,129,128]{2,1,0:T(8,128)}, f32[16,129,128]{2,1,0:T(8,128)S(1)}, u32[]{:S(2)}) copy-start(f32[16,129,128]{2,1,0:T(8,128)S(1)} %get-tuple-element.60) | copy-start | bytes 3170308
  149.9 8.7 %copy-start.9 = (f32[262144]{0:T(1024)}, f32[262144]{0:T(1024)S(1)}, u32[]{:S(2)}) copy-start(f32[262144]{0:T(1024)S(1)} %fusion.52) | copy-start | bytes 3145732
  149.9 17.8 %collective-permute-start.6 = (f32[1,128,128]{2,1,0:T(8,128)S(1)}, f32[1,128,128]{2,1,0:T(8,128)S(1)}, u32[]{:S(2)}, u32[]{:S(2)}) collective-permute-start(f32[1,128,128]{2,1,0:T(8,128)S(1)} %get-tuple-element.79), channel_id=1, source_target_pairs={{1,0},{2,1},{3,2},{4,3},{5,4},{6,5},{7,6},{9,8},{10,9},{11,10},{12... | collective-permute-start | bytes 196616 | tf_op jit(solution)/shard_map/ppermute | solution.py:17
  151.2 16.5 %collective-permute-start.7 = (f32[1,128,128]{2,1,0:T(8,128)S(1)}, f32[1,128,128]{2,1,0:T(8,128)S(1)}, u32[]{:S(2)}, u32[]{:S(2)}) collective-permute-start(f32[1,128,128]{2,1,0:T(8,128)S(1)} %get-tuple-element.78), channel_id=1, source_target_pairs={{0,1},{1,2},{2,3},{3,4},{4,5},{5,6},{6,7},{8,9},{9,10},{10,11},{11... | collective-permute-start | bytes 196616 | tf_op jit(solution)/shard_map/ppermute | solution.py:16
  175.6 8.6 %copy-start.12 = (f32[262144]{0:T(1024)}, f32[262144]{0:T(1024)S(1)}, u32[]{:S(2)}) copy-start(f32[262144]{0:T(1024)S(1)} %fusion.53) | copy-start | bytes 3145732
  175.6 17.6 %collective-permute-start.8 = (f32[1,128,128]{2,1,0:T(8,128)S(1)}, f32[1,128,128]{2,1,0:T(8,128)S(1)}, u32[]{:S(2)}, u32[]{:S(2)}) collective-permute-start(f32[1,128,128]{2,1,0:T(8,128)S(1)} %get-tuple-element.77), channel_id=1, source_target_pairs={{1,0},{2,1},{3,2},{4,3},{5,4},{6,5},{7,6},{9,8},{10,9},{11,10},{12... | collective-permute-start | bytes 196616 | tf_op jit(solution)/shard_map/ppermute | solution.py:17
  176.9 16.3 %collective-permute-start.9 = (f32[1,128,128]{2,1,0:T(8,128)S(1)}, f32[1,128,128]{2,1,0:T(8,128)S(1)}, u32[]{:S(2)}, u32[]{:S(2)}) collective-permute-start(f32[1,128,128]{2,1,0:T(8,128)S(1)} %get-tuple-element.76), channel_id=1, source_target_pairs={{0,1},{1,2},{2,3},{3,4},{4,5},{5,6},{6,7},{8,9},{9,10},{10,11},{11... | collective-permute-start | bytes 196616 | tf_op jit(solution)/shard_map/ppermute | solution.py:16
  193.2 2.5 copy-start.30
  201.1 8.7 %copy-start.15 = (f32[262144]{0:T(1024)}, f32[262144]{0:T(1024)S(1)}, u32[]{:S(2)}) copy-start(f32[262144]{0:T(1024)S(1)} %fusion.54) | copy-start | bytes 3145732
  201.1 17.8 %collective-permute-start.10 = (f32[1,128,128]{2,1,0:T(8,128)S(1)}, f32[1,128,128]{2,1,0:T(8,128)S(1)}, u32[]{:S(2)}, u32[]{:S(2)}) collective-permute-start(f32[1,128,128]{2,1,0:T(8,128)S(1)} %get-tuple-element.75), channel_id=1, source_target_pairs={{1,0},{2,1},{3,2},{4,3},{5,4},{6,5},{7,6},{9,8},{10,9},{11,10},{12... | collective-permute-start | bytes 196616 | tf_op jit(solution)/shard_map/ppermute | solution.py:17
  202.4 16.5 %collective-permute-start.11 = (f32[1,128,128]{2,1,0:T(8,128)S(1)}, f32[1,128,128]{2,1,0:T(8,128)S(1)}, u32[]{:S(2)}, u32[]{:S(2)}) collective-permute-start(f32[1,128,128]{2,1,0:T(8,128)S(1)} %get-tuple-element.74), channel_id=1, source_target_pairs={{0,1},{1,2},{2,3},{3,4},{4,5},{5,6},{6,7},{8,9},{9,10},{10,11},{11... | collective-permute-start | bytes 196616 | tf_op jit(solution)/shard_map/ppermute | solution.py:16
  218.9 2.5 copy-start.29
  221.4 5.1 %copy-start.5 = (f32[16,129,128]{2,1,0:T(8,128)S(1)}, f32[16,129,128]{2,1,0:T(8,128)}, u32[]{:S(2)}) copy-start(f32[16,129,128]{2,1,0:T(8,128)} %copy-done.2) | copy-start | bytes 3170308
  229.8 15.4 %copy-start.39 = (f32[1,1,512]{2,1,0:T(1,128)S(1)}, f32[1,1,512]{2,1,0:T(1,128)}, u32[]{:S(2)}) copy-start(f32[1,1,512]{2,1,0:T(1,128)} %get-tuple-element.84) | copy-start | bytes 6148
  229.8 15.4 %copy-start.40 = (f32[1,1,512]{2,1,0:T(1,128)S(1)}, f32[1,1,512]{2,1,0:T(1,128)}, u32[]{:S(2)}) copy-start(f32[1,1,512]{2,1,0:T(1,128)} %get-tuple-element.85) | copy-start | bytes 6148
  229.8 15.4 %copy-start.41 = (f32[512]{0:T(512)S(1)}, f32[512]{0:T(512)}, u32[]{:S(2)}) copy-start(f32[512]{0:T(512)} %gather_fusion.3) | copy-start | bytes 6148
  229.8 15.4 %copy-start.42 = (f32[512]{0:T(512)S(1)}, f32[512]{0:T(512)}, u32[]{:S(2)}) copy-start(f32[512]{0:T(512)} %gather_fusion.2) | copy-start | bytes 6148
  229.8 15.4 %copy-start.43 = (f32[512]{0:T(512)S(1)}, f32[512]{0:T(512)}, u32[]{:S(2)}) copy-start(f32[512]{0:T(512)} %gather_fusion.1) | copy-start | bytes 6148
  229.8 15.4 %copy-start.46 = (pred[512]{0:T(512)(128)(4,1)S(1)}, pred[512]{0:T(512)(128)(4,1)}, u32[]{:S(2)}) copy-start(pred[512]{0:T(512)(128)(4,1)} %and_reduce_fusion) | copy-start | bytes 1540
  238.7 6.7 %collective-permute-start.2 = (f32[1,128,128]{2,1,0:T(8,128)S(1)}, f32[1,128,128]{2,1,0:T(8,128)S(1)}, u32[]{:S(2)}, u32[]{:S(2)}) collective-permute-start(f32[1,128,128]{2,1,0:T(8,128)S(1)} %get-tuple-element.81), channel_id=1, source_target_pairs={{1,0},{2,1},{3,2},{4,3},{5,4},{6,5},{7,6},{9,8},{10,9},{11,10},{12... | collective-permute-start | bytes 196616 | tf_op jit(solution)/shard_map/ppermute | solution.py:17
  240.0 7.0 %collective-permute-start.3 = (f32[1,128,128]{2,1,0:T(8,128)S(1)}, f32[1,128,128]{2,1,0:T(8,128)S(1)}, u32[]{:S(2)}, u32[]{:S(2)}) collective-permute-start(f32[1,128,128]{2,1,0:T(8,128)S(1)} %get-tuple-element.80), channel_id=1, source_target_pairs={{0,1},{1,2},{2,3},{3,4},{4,5},{5,6},{6,7},{8,9},{9,10},{10,11},{11... | collective-permute-start | bytes 196616 | tf_op jit(solution)/shard_map/ppermute | solution.py:16
  245.3 3.7 copy-start.28
  245.3 3.7 copy-start.34
  259.4 7.4 %copy-start.6 = (f32[16,129,128]{2,1,0:T(8,128)S(1)}, f32[16,129,128]{2,1,0:T(8,128)}, u32[]{:S(2)}) copy-start(f32[16,129,128]{2,1,0:T(8,128)} %copy-done.2) | copy-start | bytes 3170308
  260.1 7.1 %collective-permute-start.12 = (f32[1,128,128]{2,1,0:T(8,128)S(1)}, f32[1,128,128]{2,1,0:T(8,128)S(1)}, u32[]{:S(2)}, u32[]{:S(2)}) collective-permute-start(f32[1,128,128]{2,1,0:T(8,128)S(1)} %get-tuple-element.73), channel_id=1, source_target_pairs={{1,0},{2,1},{3,2},{4,3},{5,4},{6,5},{7,6},{9,8},{10,9},{11,10},{12... | collective-permute-start | bytes 196616 | tf_op jit(solution)/shard_map/ppermute | solution.py:17
  261.4 7.3 %collective-permute-start.13 = (f32[1,128,128]{2,1,0:T(8,128)S(1)}, f32[1,128,128]{2,1,0:T(8,128)S(1)}, u32[]{:S(2)}, u32[]{:S(2)}) collective-permute-start(f32[1,128,128]{2,1,0:T(8,128)S(1)} %get-tuple-element.72), channel_id=1, source_target_pairs={{0,1},{1,2},{2,3},{3,4},{4,5},{5,6},{6,7},{8,9},{9,10},{10,11},{11... | collective-permute-start | bytes 196616 | tf_op jit(solution)/shard_map/ppermute | solution.py:16
  277.9 8.0 %copy-start.7 = (f32[16,129,128]{2,1,0:T(8,128)S(1)}, f32[16,129,128]{2,1,0:T(8,128)}, u32[]{:S(2)}) copy-start(f32[16,129,128]{2,1,0:T(8,128)} %copy-done.2) | copy-start | bytes 3170308
  278.6 7.5 %collective-permute-start.14 = (f32[1,128,128]{2,1,0:T(8,128)S(1)}, f32[1,128,128]{2,1,0:T(8,128)S(1)}, u32[]{:S(2)}, u32[]{:S(2)}) collective-permute-start(f32[1,128,128]{2,1,0:T(8,128)S(1)} %get-tuple-element.71), channel_id=1, source_target_pairs={{1,0},{2,1},{3,2},{4,3},{5,4},{6,5},{7,6},{9,8},{10,9},{11,10},{12... | collective-permute-start | bytes 196616 | tf_op jit(solution)/shard_map/ppermute | solution.py:17
  279.9 7.7 %collective-permute-start.15 = (f32[1,128,128]{2,1,0:T(8,128)S(1)}, f32[1,128,128]{2,1,0:T(8,128)S(1)}, u32[]{:S(2)}, u32[]{:S(2)}) collective-permute-start(f32[1,128,128]{2,1,0:T(8,128)S(1)} %get-tuple-element.70), channel_id=1, source_target_pairs={{0,1},{1,2},{2,3},{3,4},{4,5},{5,6},{6,7},{8,9},{9,10},{10,11},{11... | collective-permute-start | bytes 196616 | tf_op jit(solution)/shard_map/ppermute | solution.py:16
  296.8 7.8 %copy-start.8 = (f32[16,129,128]{2,1,0:T(8,128)S(1)}, f32[16,129,128]{2,1,0:T(8,128)}, u32[]{:S(2)}) copy-start(f32[16,129,128]{2,1,0:T(8,128)} %copy-done.2) | copy-start | bytes 3170308
  297.5 7.4 %collective-permute-start.16 = (f32[1,128,128]{2,1,0:T(8,128)S(1)}, f32[1,128,128]{2,1,0:T(8,128)S(1)}, u32[]{:S(2)}, u32[]{:S(2)}) collective-permute-start(f32[1,128,128]{2,1,0:T(8,128)S(1)} %get-tuple-element.69), channel_id=1, source_target_pairs={{1,0},{2,1},{3,2},{4,3},{5,4},{6,5},{7,6},{9,8},{10,9},{11,10},{12... | collective-permute-start | bytes 196616 | tf_op jit(solution)/shard_map/ppermute | solution.py:17
  298.8 7.7 %collective-permute-start.17 = (f32[1,128,128]{2,1,0:T(8,128)S(1)}, f32[1,128,128]{2,1,0:T(8,128)S(1)}, u32[]{:S(2)}, u32[]{:S(2)}) collective-permute-start(f32[1,128,128]{2,1,0:T(8,128)S(1)} %get-tuple-element.68), channel_id=1, source_target_pairs={{0,1},{1,2},{2,3},{3,4},{4,5},{5,6},{6,7},{8,9},{9,10},{10,11},{11... | collective-permute-start | bytes 196616 | tf_op jit(solution)/shard_map/ppermute | solution.py:16
  308.2 5.3 %copy-start.20 = (f32[262144]{0:T(1024)S(1)}, f32[262144]{0:T(1024)}, u32[]{:S(2)}) copy-start(f32[262144]{0:T(1024)} %scatter_fusion) | copy-start | bytes 3145732
  335.7 84.8 %copy-start.1 = (s32[16,2]{0,1:T(2,128)S(1)}, s32[16,2]{0,1:T(2,128)}, u32[]{:S(2)}) copy-start(s32[16,2]{0,1:T(2,128)} %param.19) | copy-start | bytes 388
  (19 other events, 36.2 us)
Sparse Core Ops, SparseCore 0:
  334.3 86.1 reduce-scatter.1
